TPU v7x, 32 devices: a whole 2x2x4 slice. The times are simulated.
32 devices in a mesh: con: 4 (over z), grid: 8 (over y, x, core).
Axes of the slice: x: 2, y: 2, z: 4, core: 2. Of those that a mesh axis runs over, the one named last changes fastest.
Arguments:
- velocity: bfloat16 [8, 2, 512, 512], P('con', None, 'grid'), may hold values from -6 to 6
- seed_adjoint: bfloat16 [8, 2, 512, 512], P('con', None, 'grid'), may hold values from -6 to 6
- land_mask: int32 [512, 512], P('grid'), may hold values from 0 to 2
- inv_x: bfloat16 [4, 128, 128], replicated, may hold values from -0.5 to 0.5
- inv_y: bfloat16 [4, 128, 128], replicated, may hold values from -0.5 to 0.5
- weights: float32 [8], P('con'), may hold values from 0.05 to 0.5
Outputs:
- velocity_adjoint: float32 [8, 2, 512, 512], P('con', None, 'grid')
Inputs may be any that keep to these rules, and one draw needn't show every extreme that they name: `land_mask`: 0 marks land, 1 a wet interior cell, 2 an open-boundary cell whose value is prescribed.
All inputs are finite; a program needn't handle non-finite values.
Results may differ from a plain program's by a relative error of at most 0.0039.
Values may be sent and summed in bfloat16 or wider, within the bound.
A program may use at most 64 MiB of HBM per device.

v0:
```python
import jax
import jax.numpy as jnp
from jax import lax
from jax.sharding import PartitionSpec as P

BLK = 128


def local(velocity, seed_adjoint, land_mask, inv_x, inv_y, weights):
    nblocks = inv_x.shape[0]
    con_local = velocity.shape[0]
    cols_local = seed_adjoint.shape[2]
    full_side = seed_adjoint.shape[3]
    rows_local = velocity.shape[2]
    vel_float = velocity.astype(jnp.float32)
    weight_full = weights[:, None, None, None]
    local_squares = jnp.sum(weight_full * vel_float * vel_float, axis=(0, 1))
    squares = lax.psum(local_squares, "con")
    sea_bool = land_mask == 1
    sea_float = sea_bool.astype(jnp.float32)
    sea_turned = jnp.swapaxes(sea_bool, 0, 1).astype(jnp.bfloat16)
    blocks_x = seed_adjoint.reshape(con_local, 2, cols_local, nblocks, BLK)
    across = jnp.einsum("cpyki,kji->cpykj", blocks_x, inv_x, preferred_element_type=jnp.float32)
    across = across.astype(jnp.bfloat16).reshape(con_local, 2, cols_local, full_side)
    arrived = lax.all_to_all(across, "grid", split_axis=3, concat_axis=2, tiled=True)
    count = arrived.shape[0]
    masked = arrived * sea_turned[None, None]
    blocks_y = masked.reshape(count, 2, nblocks, BLK, rows_local)
    solved = jnp.einsum("cpkiu,kji->cpukj", blocks_y, inv_y, preferred_element_type=jnp.float32)
    rhs_adjoint = solved.reshape(count, 2, rows_local, nblocks * BLK)
    local_inner = jnp.sum(rhs_adjoint * vel_float, axis=(0, 1))
    inner = lax.psum(local_inner.astype(jnp.bfloat16), "con").astype(jnp.float32)
    speed = jnp.sqrt(0.25 + squares)
    first = -0.5 * sea_float * speed * rhs_adjoint
    second = -0.5 * sea_float * weight_full * vel_float * inner / speed
    return first + second


def solution(mesh):
    return jax.shard_map(
        local,
        mesh=mesh,
        in_specs=(
            P("con", None, "grid", None),
            P("con", None, "grid", None),
            P("grid", None),
            P(),
            P(),
            P("con"),
        ),
        out_specs=P("con", None, "grid", None),
        check_vma=False,
    )
```

profile of v0, /device:TPU:0, one launch (start us, length us, event | category | flops | bytes accessed | tf_op | source)
XLA Modules:
  0.0 104.8 jit_solution(13797444481957824406)
XLA Ops:
  6.5 0.0 copy-start
  6.5 0.9 copy-done
  7.5 1.1 %fusion = bf16[2,2,64,4,128]{4,2,1,0,3:T(8,128)(2,1)S(1)} fusion(bf16[4,128,128]{2,1,0:T(8,128)(2,1)} %param.9, bf16[2,2,64,512]{3,2,1,0:T(8,128)(2,1)S(1)} %copy-done), kind=kOutput, calls=%fused_computation.2 | convolution fusion | flops 33685504 | bytes 655360 | tf_op jit(solution)/shard_map/cpyki,kji->cpykj/dot_general | solution.py:23
  8.6 0.4 copy.22
  9.0 1.1 %reshape.31 = bf16[8,2,8192]{2,1,0:T(2,128)(2,1)} reshape(bf16[512,2,2,64]{3,2,1,0:T(2,128)(2,1)S(1)} %bitcast.45) | data formatting | bytes 524288
  10.1 0.0 copy-start.3
  10.1 5.3 %all-to-all-start = ((bf16[8,2,8192]{2,1,0:T(2,128)(2,1)}), bf16[8,2,8192]{2,1,0:T(2,128)(2,1)S(1)}, u32[]{:S(2)}, u32[]{:S(2)}) async-start(bf16[8,2,8192]{2,1,0:T(2,128)(2,1)} %reshape.31), calls=%async_computation | async-start | bytes 524288 | tf_op jit(solution)/shard_map/all_to_all | solution.py:25
  15.4 0.0 all-reduce.5.cloned.1.call-start
  15.5 0.0 copy-done.3
  15.6 6.8 %all-to-all-done = bf16[8,2,8192]{2,1,0:T(2,128)(2,1)S(1)} async-done(((bf16[8,2,8192]{2,1,0:T(2,128)(2,1)}), bf16[8,2,8192]{2,1,0:T(2,128)(2,1)S(1)}, u32[]{:S(2)}, u32[]{:S(2)}) %all-to-all-start) | async-done | bytes 262176 | tf_op jit(solution)/shard_map/all_to_all | solution.py:25
  22.4 0.3 reshape.32
  22.7 0.3 copy.35
  23.1 0.2 all_to_all.16
  23.3 0.0 copy-start.2
  23.4 0.9 copy-done.2
  24.2 0.0 copy-start.1
  24.2 0.0 copy-start.4
  24.2 0.2 convolution_bitcast_fusion
  24.5 0.7 copy-done.1
  25.2 0.0 copy-done.4
  25.2 0.8 fusion.5
  26.0 0.0 all-reduce.5.cloned.1.call-update
  26.0 0.0 all-reduce.3.cloned.1.call-start
  26.0 0.7 all-reduce.3.cloned.1.call-update
  26.7 0.1 broadcast_multiply_fusion
  26.8 32.7 %all-reduce.5.cloned.1.call-done = bf16[64,512]{1,0:T(8,128)(2,1)} async-done(((bf16[64,512]{1,0:T(8,128)(2,1)}), bf16[64,512]{1,0:T(8,128)(2,1)}) %all-reduce.5.cloned.1.call-update) | async-done | bytes 65552 | tf_op jit(solution)/shard_map/psum | solution.py:32
  59.5 0.8 convert_element_type.25
  60.3 35.8 %all-reduce.3.cloned.1.call-done = f32[64,512]{1,0:T(8,128)} async-done(((f32[64,512]{1,0:T(8,128)}), f32[64,512]{1,0:T(8,128)}) %all-reduce.3.cloned.1.call-update) | async-done | bytes 131088 | tf_op jit(solution)/shard_map/psum | solution.py:18
  96.1 1.0 fusion.11
  97.1 0.9 fusion.4
  (4 shorter events, 0.1 us)
Async XLA Ops:
  6.5 1.0 copy-start
  10.1 5.4 %copy-start.3 = (s32[64,512]{1,0:T(8,128)S(1)}, s32[64,512]{1,0:T(8,128)}, u32[]{:S(2)}) copy-start(s32[64,512]{1,0:T(8,128)} %param.8) | copy-start | bytes 393220
  10.1 12.2 %all-to-all-start = ((bf16[8,2,8192]{2,1,0:T(2,128)(2,1)}), bf16[8,2,8192]{2,1,0:T(2,128)(2,1)S(1)}, u32[]{:S(2)}, u32[]{:S(2)}) async-start(bf16[8,2,8192]{2,1,0:T(2,128)(2,1)} %reshape.31), calls=%async_computation | async-start | bytes 524288 | tf_op jit(solution)/shard_map/all_to_all | solution.py:25
  15.4 44.1 %all-reduce.5.cloned.1.call-start = ((), (), s32[]{:S(2)}) async-start(), calls=%async_computation.2 | async-start | bytes 131072 | tf_op jit(solution)/shard_map/psum | solution.py:32
  23.3 0.9 copy-start.2
  24.2 0.9 copy-start.1
  24.2 1.0 copy-start.4
  26.0 70.1 %all-reduce.3.cloned.1.call-start = ((), (), s32[]{:S(2)}) async-start(), calls=%async_computation.1 | async-start | bytes 262144 | tf_op jit(solution)/shard_map/psum | solution.py:18
Sparse Core Ops, SparseCore 0:
  26.1 33.3 all-reduce.4
  61.9 34.1 all-reduce.2
where the time goes:
time: 105 us
  waiting for transfers between devices  76 us (72%)
  between operations  13.5 us (13%)
  starting transfers between devices  5.38 us (5%)
  local copies, waits for them, and re-layouts  5 us (5%)
  other arithmetic  3.65 us (3%)
  matrix products  1.36 us (1%)
    psum x1, waiting for transfers between devices, local(): squares = lax.psum(local_squares, 'con')  35.8 us
    psum x1, waiting for transfers between devices, local(): lax.psum(local_inner.astype(jnp.bfloat16), 'con').astype(jnp.float32)  32.7 us
    all_to_all x1, waiting for transfers between devices, local(): lax.all_to_all(across, 'grid', split_axis=3, concat_axis=2, tiled=True)  6.81 us
    all_to_all x1, starting transfers between devices, local(): lax.all_to_all(across, 'grid', split_axis=3, concat_axis=2, tiled=True)  5.3 us
    unnamed x12, local copies, waits for them, and re-layouts  3.98 us
  transfers between devices with their start and end apart: 3, of which 3 were waited for; matrix products, arithmetic and copies ran while one was open for 1% of the time, Pallas kernels for 0%

commit v1 on v0

v1 whole, which is shorter than its diff:
```python
import functools
import jax
import jax.numpy as jnp
from jax import lax
from jax.experimental import pallas as pl
from jax.experimental.pallas import tpu as pltpu
from jax.sharding import PartitionSpec as P

BLK = 128
MESH = pl.DeviceIdType.MESH
F32, BF16 = jnp.float32, jnp.bfloat16
LAST = (((1,), (1,)), ((), ()))


def partner(own, step, count):
    if count & (count - 1):
        return lax.rem(own + step, count)
    total, bit = 0, 1
    while bit < count:
        mine = lax.rem(lax.div(own, bit), 2)
        turn = step // bit % 2 if isinstance(step, int) else lax.rem(lax.div(step, bit), 2)
        total = total + lax.rem(mine + turn, 2) * bit
        bit *= 2
    return total


def steps(first, stop, body):
    if stop - first <= 8:
        for step in range(first, stop):
            body(step)
    else:
        @pl.loop(first, stop)
        def _(step):
            body(step)


def lanes(block):
    return pl.ds(pl.multiple_of(block * BLK, BLK), BLK)


def kernel(
    dims,
    vel_hbm, seed_hbm, land_hbm, ix_hbm, iy_hbm, w_ref,
    out_ref,
    vel, seed, land, ix, iy,
    send, recv, wide, mask,
    sq_part, sq_send, sq_rs, sq_ag,
    rhs, in_part, in_send, in_rs, in_ag, ca, cb,
    load_sem, a2a_send, a2a_recv, sq_send_sem, sq_recv_sem, in_send_sem, in_recv_sem,
):
    n_con, n_grid, n_blk, con_local, rows, side = dims
    pack = BLK // rows
    n_cp = con_local * 2
    groups = n_cp // pack
    share = rows // n_con
    me = lax.axis_index("grid")
    zc = lax.axis_index("con")
    own = lax.div(me, pack)
    core = lax.rem(me, pack)

    loads = []
    for i, (src, dst) in enumerate(((seed_hbm, seed), (ix_hbm, ix), (vel_hbm, vel), (iy_hbm, iy), (land_hbm, land))):
        copy = pltpu.make_async_copy(src, dst, load_sem.at[i])
        copy.start()
        loads.append(copy)
    barrier = pltpu.get_barrier_semaphore()
    for d in range(1, n_grid):
        pl.semaphore_signal(barrier, inc=1, device_id={"grid": lax.rem(me + d, n_grid)}, device_id_type=MESH)
    for d in range(1, n_con):
        pl.semaphore_signal(barrier, inc=1, device_id={"con": lax.rem(zc + d, n_con)}, device_id_type=MESH)

    def a2a_copy(peer):
        return pltpu.make_async_remote_copy(
            src_ref=send.at[peer], dst_ref=recv.at[me],
            send_sem=a2a_send.at[peer], recv_sem=a2a_recv.at[me],
            device_id={"grid": peer}, device_id_type=MESH)

    def a2a_arrival(peer):
        return pltpu.make_async_remote_copy(
            src_ref=send.at[peer], dst_ref=recv.at[peer],
            send_sem=a2a_send.at[peer], recv_sem=a2a_recv.at[peer],
            device_id={"grid": peer}, device_id_type=MESH)

    def peer_in(step, slot):
        block = partner(own, step, n_blk)
        return block * pack + slot

    loads[0].wait()
    loads[1].wait()

    def solve_x(step):
        block = partner(own, step, n_blk)
        field = seed[:, :, :, lanes(block)].reshape(n_cp * rows, BLK)
        turned = lax.dot_general(ix[block], field, LAST, preferred_element_type=F32).astype(BF16)
        for half in range(pack):
            send[block * pack + half] = turned[half * rows:(half + 1) * rows]

    steps(1, n_blk, solve_x)
    solve_x(0)
    recv[me] = send[me]

    loads[2].wait()

    def square(block):
        cols = lanes(block)
        total = jnp.zeros((rows, BLK), F32)
        for c in range(con_local):
            v0 = vel[c, 0, :, cols].astype(F32)
            v1 = vel[c, 1, :, cols].astype(F32)
            total = total + w_ref[c] * (v0 * v0 + v1 * v1)
        sq_part[:, cols] = total
        sq_send[:, cols] = total.astype(BF16)

    steps(0, n_blk, square)

    pl.semaphore_wait(barrier, n_grid - 1 + n_con - 1)
    for slot in range(1, pack):
        a2a_copy(own * pack + lax.rem(core + slot, pack)).start()

    def send_step(step):
        for slot in range(pack):
            a2a_copy(peer_in(step, slot)).start()

    steps(1, n_blk, send_step)

    def share_of(index):
        return pl.ds(pl.multiple_of(index * share, share), share)

    def sq_scatter(d):
        peer = lax.rem(zc + d, n_con)
        return pltpu.make_async_remote_copy(
            src_ref=sq_send.at[share_of(peer)], dst_ref=sq_rs.at[d - 1],
            send_sem=sq_send_sem.at[0, d - 1], recv_sem=sq_recv_sem.at[0, d - 1],
            device_id={"con": peer}, device_id_type=MESH)

    def sq_gather(d):
        peer = lax.rem(zc + d, n_con)
        return pltpu.make_async_remote_copy(
            src_ref=sq_ag.at[share_of(zc)], dst_ref=sq_ag.at[share_of(zc)],
            send_sem=sq_send_sem.at[1, d - 1], recv_sem=sq_recv_sem.at[1, d - 1],
            device_id={"con": peer}, device_id_type=MESH)

    def sq_gathered(d):
        source = lax.rem(zc + n_con - d, n_con)
        return pltpu.make_async_remote_copy(
            src_ref=sq_ag.at[share_of(zc)], dst_ref=sq_ag.at[share_of(source)],
            send_sem=sq_send_sem.at[1, d - 1], recv_sem=sq_recv_sem.at[1, d - 1],
            device_id={"con": source}, device_id_type=MESH)

    for d in range(1, n_con):
        sq_scatter(d).start()

    loads[3].wait()
    loads[4].wait()
    lane = lax.broadcasted_iota(jnp.int32, (BLK, BLK), 1)
    lane_m = lax.broadcasted_iota(jnp.int32, (rows, BLK), 1)

    def spread(tile, lane_of, place, source):
        shift = (place - source) * rows % BLK
        moved = pltpu.roll(tile, shift, 1) if shift else tile
        return jnp.where(lax.div(lane_of, rows) == place, moved, 0.0)

    def prepare(block):
        tile = iy[block].astype(F32)
        sea = (land[:, lanes(block)] == 1).astype(F32)
        for source in range(pack):
            spot = slice(source * BLK, (source + 1) * BLK)
            if pack == 1:
                wide[block] = iy[block]
                mask[block] = sea.astype(BF16)
            else:
                both = jnp.zeros((rows, BLK), F32)
                for place in range(pack):
                    wide[block, place * BLK:(place + 1) * BLK, spot] = spread(tile, lane, place, source).astype(BF16)
                    both = both + spread(sea, lane_m, place, source)
                mask[block, :, spot] = both.astype(BF16)

    steps(0, n_blk, prepare)

    for d in range(1, n_con):
        sq_scatter(d).wait_recv()
    total = sq_part[share_of(zc)]
    for d in range(1, n_con):
        total = total + sq_rs[d - 1].astype(F32)
    sq_ag[share_of(zc)] = total.astype(BF16)
    for d in range(1, n_con):
        sq_gather(d).start()

    def in_scatter(step, d):
        peer = lax.rem(zc + d, n_con)
        return pltpu.make_async_remote_copy(
            src_ref=in_send.at[step, share_of(peer)], dst_ref=in_rs.at[step, d - 1],
            send_sem=in_send_sem.at[0, step, d - 1], recv_sem=in_recv_sem.at[0, step, d - 1],
            device_id={"con": peer}, device_id_type=MESH)

    def in_gather(step, d):
        peer = lax.rem(zc + d, n_con)
        return pltpu.make_async_remote_copy(
            src_ref=in_ag.at[step, share_of(zc)], dst_ref=in_ag.at[step, share_of(zc)],
            send_sem=in_send_sem.at[1, step, d - 1], recv_sem=in_recv_sem.at[1, step, d - 1],
            device_id={"con": peer}, device_id_type=MESH)

    def in_gathered(step, d):
        source = lax.rem(zc + n_con - d, n_con)
        return pltpu.make_async_remote_copy(
            src_ref=in_ag.at[step, share_of(zc)], dst_ref=in_ag.at[step, share_of(source)],
            send_sem=in_send_sem.at[1, step, d - 1], recv_sem=in_recv_sem.at[1, step, d - 1],
            device_id={"con": source}, device_id_type=MESH)

    def solve_y(step, waits):
        for peer in waits:
            a2a_arrival(peer).wait_recv()
        block = partner(own, step, n_blk)
        cols = lanes(block)
        weight = wide[block]
        keep = mask[block]
        parts = []
        for q in range(groups):
            pieces = [recv[block * pack + source, :, q * BLK:(q + 1) * BLK] for source in range(pack)]
            parts.append((pieces[0] if pack == 1 else jnp.concatenate(pieces, axis=1)) * keep)
        solved = lax.dot_general(jnp.concatenate(parts, axis=0), weight, LAST, preferred_element_type=F32)
        total = jnp.zeros((rows, BLK), F32)
        for cp in range(n_cp):
            q, place = cp // pack, cp % pack
            value = solved[q * rows:(q + 1) * rows, place * BLK:(place + 1) * BLK]
            rhs[cp, :, cols] = value
            total = total + value * vel[cp // 2, cp % 2, :, cols].astype(F32)
        in_part[step] = total
        in_send[step] = total.astype(BF16)
        for d in range(1, n_con):
            in_scatter(step, d).start()

    def reduce_inner(step):
        for d in range(1, n_con):
            in_scatter(step, d).wait_recv()
        mine = in_part[step, share_of(zc)]
        for d in range(1, n_con):
            mine = mine + in_rs[step, d - 1].astype(F32)
        in_ag[step, share_of(zc)] = mine.astype(BF16)
        for d in range(1, n_con):
            in_gather(step, d).start()

    solve_y(0, [own * pack + lax.rem(core + slot, pack) for slot in range(1, pack)])

    def step_y(step):
        solve_y(step, [peer_in(step, slot) for slot in range(pack)])
        reduce_inner(step - 1)

    steps(1, n_blk, step_y)
    reduce_inner(n_blk - 1)

    for d in range(1, n_con):
        sq_gathered(d).wait_recv()

    def factors(block):
        cols = lanes(block)
        squared = 0.25 + sq_ag[:, cols].astype(F32)
        inverse = lax.rsqrt(squared)
        half = jnp.where(land[:, cols] == 1, -0.5, 0.0)
        ca[:, cols] = half * (squared * inverse)
        cb[:, cols] = half * inverse

    steps(0, n_blk, factors)

    def finish(step):
        for d in range(1, n_con):
            in_gathered(step, d).wait_recv()
        cols = lanes(partner(own, step, n_blk))
        first = ca[:, cols]
        second = cb[:, cols] * in_ag[step].astype(F32)
        for c in range(con_local):
            scaled = w_ref[c] * second
            for p in range(2):
                out_ref[c, p, :, cols] = first * rhs[2 * c + p, :, cols] + scaled * vel[c, p, :, cols].astype(F32)

    steps(0, n_blk, finish)

    for slot in range(1, pack):
        a2a_copy(own * pack + lax.rem(core + slot, pack)).wait_send()

    def left(step):
        for slot in range(pack):
            a2a_copy(peer_in(step, slot)).wait_send()

    steps(1, n_blk, left)
    for d in range(1, n_con):
        sq_scatter(d).wait_send()
        sq_gather(d).wait_send()

    def in_left(step):
        for d in range(1, n_con):
            in_scatter(step, d).wait_send()
            in_gather(step, d).wait_send()

    steps(0, n_blk, in_left)


def local(n_con, n_grid, velocity, seed_adjoint, land_mask, inv_x, inv_y, weights):
    con_local, _, rows, side = velocity.shape
    n_blk = inv_x.shape[0]
    pack = BLK // rows
    n_cp = 2 * con_local
    dims = (n_con, n_grid, n_blk, con_local, rows, side)
    share = rows // n_con
    vm = pltpu.VMEM
    sem = pltpu.SemaphoreType.DMA
    peers = max(n_con - 1, 1)
    scratch = [
        vm(velocity.shape, BF16), vm(seed_adjoint.shape, BF16), vm(land_mask.shape, jnp.int32),
        vm(inv_x.shape, BF16), vm(inv_y.shape, BF16),
        vm((n_grid, rows, n_cp * rows), BF16), vm((n_grid, rows, n_cp * rows), BF16),
        vm((n_blk, pack * BLK, pack * BLK), BF16), vm((n_blk, rows, pack * BLK), BF16),
        vm((rows, side), F32), vm((rows, side), BF16), vm((peers, share, side), BF16), vm((rows, side), BF16),
        vm((n_cp, rows, side), F32), vm((n_blk, rows, BLK), F32), vm((n_blk, rows, BLK), BF16),
        vm((n_blk, peers, share, BLK), BF16), vm((n_blk, rows, BLK), BF16),
        vm((rows, side), F32), vm((rows, side), F32),
        sem((5,)), sem((n_grid,)), sem((n_grid,)),
        sem((2, peers)), sem((2, peers)), sem((2, n_blk, peers)), sem((2, n_blk, peers)),
    ]
    anywhere = pl.BlockSpec(memory_space=pl.ANY)
    flops = 2 * 2 * n_cp * rows * side * BLK
    return pl.pallas_call(
        functools.partial(kernel, dims),
        out_shape=jax.ShapeDtypeStruct(velocity.shape, F32),
        in_specs=[anywhere] * 5 + [pl.BlockSpec(memory_space=pltpu.SMEM)],
        out_specs=pl.BlockSpec(memory_space=pltpu.VMEM),
        scratch_shapes=scratch,
        cost_estimate=pl.CostEstimate(flops=flops, bytes_accessed=4 * velocity.size * 2, transcendentals=rows * side),
        compiler_params=pltpu.CompilerParams(
            collective_id=0, has_side_effects=True, vmem_limit_bytes=58 * 1024 * 1024),
    )(velocity, seed_adjoint, land_mask, inv_x, inv_y, weights)


def solution(mesh):
    return jax.shard_map(
        functools.partial(local, mesh.shape["con"], mesh.shape["grid"]),
        mesh=mesh,
        in_specs=(
            P("con", None, "grid", None),
            P("con", None, "grid", None),
            P("grid", None),
            P(),
            P(),
            P("con"),
        ),
        out_specs=P("con", None, "grid", None),
        check_vma=False,
    )
```

time: 105 us -> 25 us (0.24)
  waiting for transfers between devices: 76 us -> 0 us
  Pallas kernels: 0 us -> 23 us
  between operations: 13.5 us -> 0.01 us
  starting transfers between devices: 5.38 us -> 0 us
  other arithmetic: 3.65 us -> 0 us
  local copies, waits for them, and re-layouts: 5 us -> 1.87 us
  matrix products: 1.36 us -> 0 us
    psum x2 -> x0, waiting for transfers between devices: 68.4 us -> none  [the longest x1 35.8 us: local(): squares = lax.psum(local_squares, 'con')]
    pallas_call x0 -> x1, Pallas kernels: none -> 23 us  [local(): pl.pallas_call(functools.partial(kernel, dims), out_shape=jax.ShapeDtypeS...]
    all_to_all x1 -> x0, waiting for transfers between devices: 6.81 us -> none  [local(): lax.all_to_all(across, 'grid', split_axis=3, concat_axis=2, tiled=True)]
    all_to_all x1 -> x0, starting transfers between devices: 5.3 us -> none  [local(): lax.all_to_all(across, 'grid', split_axis=3, concat_axis=2, tiled=True)]
    unnamed x12 -> x1, local copies, waits for them, and re-layouts: 3.98 us -> 1.87 us
    dot_general x2 -> x0, matrix products: 1.36 us -> none  [the longest x1 1.13 us: local(): jnp.einsum('cpyki,kji->cpykj', blocks_x, inv_x, preferred_element_type=jn...]
    mul x5 -> x0, other arithmetic: 1.1 us -> none  [the longest x2 0.98 us: local(): first = -0.5 * sea_float * speed * rhs_adjoint]
  transfers between devices with their start and end apart: 3 -> 0, of which waited for: 3 -> 0; matrix products, arithmetic and copies ran while one was open for 1% -> 0% of each run, Pallas kernels for 0% -> 0%
where the time goes in v1:
time: 25 us; the launch traced here: 24.9 us
  Pallas kernels  23 us (92%)
  local copies, waits for them, and re-layouts  1.87 us (7%)
    pallas_call x1, Pallas kernels, local(): pl.pallas_call(functools.partial(kernel, dims), out_shape=jax.ShapeDtypeS...  23 us
    unnamed x1, local copies, waits for them, and re-layouts  1.87 us

profile of v1, /device:TPU:0, one launch (start us, length us, event | category | flops | bytes accessed | tf_op | source)
XLA Modules:
  0.0 24.9 jit_solution(12499811606353851141)
XLA Ops:
  0.0 23.0 %shard_map.64 = f32[2,2,64,512]{3,2,1,0:T(8,128)} custom-call(bf16[2,2,64,512]{3,2,1,0:T(8,128)(2,1)} %vel_hbm.1, bf16[2,2,64,512]{3,2,1,0:T(8,128)(2,1)} %seed_hbm.1, s32[64,512]{1,0:T(8,128)} %land_hbm.1, bf16[4,128,128]{2,1,0:T(8,128)(2,1)} %ix_hbm.1, bf16[4,128,128]{2,1,0:T(8,128)(2,1)} %iy_hbm.1, f32[2]{0:T(128)} %w_ref.1), custom_call_target="tpu_custom_call" | custom-call | flops 67108864 | bytes 1048576 | tf_op jit(solution)/shard_map/pallas_call | solution.py:322
  23.0 1.9 %copy.8 = f32[2,2,64,512]{3,2,1,0:T(8,128)} copy(f32[2,2,64,512]{3,2,1,0:T(8,128)} %shard_map.64) | data formatting | bytes 1048576

commit v2 on v1

--- a/solution.py
+++ b/solution.py
@@ -1,4 +1,5 @@
 import functools
+import math
 import jax
 import jax.numpy as jnp
 from jax import lax
@@ -40,9 +41,9 @@
 
 def kernel(
     dims,
-    vel_hbm, seed_hbm, land_hbm, ix_hbm, iy_hbm, w_ref,
+    vel_hbm, seed_hbm, land_hbm, ix_hbm, iy_hbm, w_hbm,
     out_ref,
-    vel, seed, land, ix, iy,
+    vel, seed, land, ix, iy, w_ref,
     send, recv, wide, mask,
     sq_part, sq_send, sq_rs, sq_ag,
     rhs, in_part, in_send, in_rs, in_ag, ca, cb,
@@ -58,16 +59,17 @@
     own = lax.div(me, pack)
     core = lax.rem(me, pack)
 
+    barrier = pltpu.get_barrier_semaphore()
+    for d in range(1, n_grid):
+        pl.semaphore_signal(barrier, inc=1, device_id={"grid": lax.rem(me + d, n_grid)}, device_id_type=MESH)
+    for d in range(1, n_con):
+        pl.semaphore_signal(barrier, inc=1, device_id={"con": lax.rem(zc + d, n_con)}, device_id_type=MESH)
+
     loads = []
-    for i, (src, dst) in enumerate(((seed_hbm, seed), (ix_hbm, ix), (vel_hbm, vel), (iy_hbm, iy), (land_hbm, land))):
+    for i, (src, dst) in enumerate(((seed_hbm, seed), (ix_hbm, ix), (vel_hbm, vel), (w_hbm, w_ref), (iy_hbm, iy), (land_hbm, land))):
         copy = pltpu.make_async_copy(src, dst, load_sem.at[i])
         copy.start()
         loads.append(copy)
-    barrier = pltpu.get_barrier_semaphore()
-    for d in range(1, n_grid):
-        pl.semaphore_signal(barrier, inc=1, device_id={"grid": lax.rem(me + d, n_grid)}, device_id_type=MESH)
-    for d in range(1, n_con):
-        pl.semaphore_signal(barrier, inc=1, device_id={"con": lax.rem(zc + d, n_con)}, device_id_type=MESH)
 
     def a2a_copy(peer):
         return pltpu.make_async_remote_copy(
@@ -95,11 +97,21 @@
         for half in range(pack):
             send[block * pack + half] = turned[half * rows:(half + 1) * rows]
 
-    steps(1, n_blk, solve_x)
+    pl.semaphore_wait(barrier, n_grid - 1 + n_con - 1)
+
+    def solve_and_send(step):
+        solve_x(step)
+        for slot in range(pack):
+            a2a_copy(peer_in(step, slot)).start()
+
+    steps(1, n_blk, solve_and_send)
     solve_x(0)
+    for slot in range(1, pack):
+        a2a_copy(own * pack + lax.rem(core + slot, pack)).start()
     recv[me] = send[me]
 
     loads[2].wait()
+    loads[3].wait()
 
     def square(block):
         cols = lanes(block)
@@ -113,16 +125,6 @@
 
     steps(0, n_blk, square)
 
-    pl.semaphore_wait(barrier, n_grid - 1 + n_con - 1)
-    for slot in range(1, pack):
-        a2a_copy(own * pack + lax.rem(core + slot, pack)).start()
-
-    def send_step(step):
-        for slot in range(pack):
-            a2a_copy(peer_in(step, slot)).start()
-
-    steps(1, n_blk, send_step)
-
     def share_of(index):
         return pl.ds(pl.multiple_of(index * share, share), share)
 
@@ -150,8 +152,8 @@
     for d in range(1, n_con):
         sq_scatter(d).start()
 
-    loads[3].wait()
     loads[4].wait()
+    loads[5].wait()
     lane = lax.broadcasted_iota(jnp.int32, (BLK, BLK), 1)
     lane_m = lax.broadcasted_iota(jnp.int32, (rows, BLK), 1)
 
@@ -307,27 +309,29 @@
     peers = max(n_con - 1, 1)
     scratch = [
         vm(velocity.shape, BF16), vm(seed_adjoint.shape, BF16), vm(land_mask.shape, jnp.int32),
-        vm(inv_x.shape, BF16), vm(inv_y.shape, BF16),
+        vm(inv_x.shape, BF16), vm(inv_y.shape, BF16), pltpu.SMEM(weights.shape, F32),
         vm((n_grid, rows, n_cp * rows), BF16), vm((n_grid, rows, n_cp * rows), BF16),
         vm((n_blk, pack * BLK, pack * BLK), BF16), vm((n_blk, rows, pack * BLK), BF16),
         vm((rows, side), F32), vm((rows, side), BF16), vm((peers, share, side), BF16), vm((rows, side), BF16),
         vm((n_cp, rows, side), F32), vm((n_blk, rows, BLK), F32), vm((n_blk, rows, BLK), BF16),
         vm((n_blk, peers, share, BLK), BF16), vm((n_blk, rows, BLK), BF16),
         vm((rows, side), F32), vm((rows, side), F32),
-        sem((5,)), sem((n_grid,)), sem((n_grid,)),
+        sem((6,)), sem((n_grid,)), sem((n_grid,)),
         sem((2, peers)), sem((2, peers)), sem((2, n_blk, peers)), sem((2, n_blk, peers)),
     ]
-    anywhere = pl.BlockSpec(memory_space=pl.ANY)
+    held = sum(math.prod(spec.shape) * jnp.dtype(spec.dtype).itemsize for spec in scratch[:21])
+    limit = held + velocity.size * 4 + max(4 << 20, velocity.size * 4)
+    anywhere = pl.BlockSpec(memory_space=pltpu.HBM)
     flops = 2 * 2 * n_cp * rows * side * BLK
     return pl.pallas_call(
         functools.partial(kernel, dims),
         out_shape=jax.ShapeDtypeStruct(velocity.shape, F32),
-        in_specs=[anywhere] * 5 + [pl.BlockSpec(memory_space=pltpu.SMEM)],
+        in_specs=[anywhere] * 6,
         out_specs=pl.BlockSpec(memory_space=pltpu.VMEM),
         scratch_shapes=scratch,
         cost_estimate=pl.CostEstimate(flops=flops, bytes_accessed=4 * velocity.size * 2, transcendentals=rows * side),
         compiler_params=pltpu.CompilerParams(
-            collective_id=0, has_side_effects=True, vmem_limit_bytes=58 * 1024 * 1024),
+            collective_id=0, has_side_effects=True, vmem_limit_bytes=limit),
     )(velocity, seed_adjoint, land_mask, inv_x, inv_y, weights)
 
 

time: 25 us -> 28.6 us (1.14)
  local copies, waits for them, and re-layouts: 1.87 us -> 6.06 us
  Pallas kernels: 23 us -> 22.3 us
    unnamed x1 -> x13, local copies, waits for them, and re-layouts: 1.87 us -> 6.06 us
    pallas_call x1, Pallas kernels: 23 us -> 22.3 us  [local(): pl.pallas_call(functools.partial(kernel, dims), out_shape=jax.ShapeDtypeS...]
where the time goes in v2:
time: 28.6 us; the launch traced here: 28.4 us
  Pallas kernels  22.3 us (78%)
  local copies, waits for them, and re-layouts  6.06 us (21%)
    pallas_call x1, Pallas kernels, local(): pl.pallas_call(functools.partial(kernel, dims), out_shape=jax.ShapeDtypeS...  22.3 us
    unnamed x13, local copies, waits for them, and re-layouts  6.06 us

profile of v2, /device:TPU:0, one launch (start us, length us, event | category | flops | bytes accessed | tf_op | source)
XLA Modules:
  0.0 28.4 jit_solution(14994823520822720305)
XLA Ops:
  0.0 0.0 copy-start
  0.0 0.9 %copy-done = bf16[2,2,64,512]{3,2,1,0:T(8,128)(2,1)S(1)} copy-done((bf16[2,2,64,512]{3,2,1,0:T(8,128)(2,1)S(1)}, bf16[2,2,64,512]{3,2,1,0:T(8,128)(2,1)}, u32[]{:S(2)}) %copy-start) | copy-done | bytes 262168
  1.0 0.0 copy-start.1
  1.0 0.9 %copy-done.1 = bf16[2,2,64,512]{3,2,1,0:T(8,128)(2,1)S(1)} copy-done((bf16[2,2,64,512]{3,2,1,0:T(8,128)(2,1)S(1)}, bf16[2,2,64,512]{3,2,1,0:T(8,128)(2,1)}, u32[]{:S(2)}) %copy-start.1) | copy-done | bytes 262168
  1.9 0.0 copy-start.2
  1.9 0.9 %copy-done.2 = s32[64,512]{1,0:T(8,128)S(1)} copy-done((s32[64,512]{1,0:T(8,128)S(1)}, s32[64,512]{1,0:T(8,128)}, u32[]{:S(2)}) %copy-start.2) | copy-done | bytes 131096
  2.8 0.0 copy-start.3
  2.8 0.9 %copy-done.3 = bf16[4,128,128]{2,1,0:T(8,128)(2,1)S(1)} copy-done((bf16[4,128,128]{2,1,0:T(8,128)(2,1)S(1)}, bf16[4,128,128]{2,1,0:T(8,128)(2,1)}, u32[]{:S(2)}) %copy-start.3) | copy-done | bytes 131096
  3.7 0.0 copy-start.4
  3.7 0.9 %copy-done.4 = bf16[4,128,128]{2,1,0:T(8,128)(2,1)S(1)} copy-done((bf16[4,128,128]{2,1,0:T(8,128)(2,1)S(1)}, bf16[4,128,128]{2,1,0:T(8,128)(2,1)}, u32[]{:S(2)}) %copy-start.4) | copy-done | bytes 131096
  4.6 0.0 copy-start.5
  4.6 0.7 %copy-done.5 = f32[2]{0:T(128)S(1)} copy-done((f32[2]{0:T(128)S(1)}, f32[2]{0:T(128)}, u32[]{:S(2)}) %copy-start.5) | copy-done | bytes 32
  5.3 22.3 %shard_map.64 = f32[2,2,64,512]{3,2,1,0:T(8,128)S(1)} custom-call(bf16[2,2,64,512]{3,2,1,0:T(8,128)(2,1)S(1)} %copy-done, bf16[2,2,64,512]{3,2,1,0:T(8,128)(2,1)S(1)} %copy-done.1, s32[64,512]{1,0:T(8,128)S(1)} %copy-done.2, bf16[4,128,128]{2,1,0:T(8,128)(2,1)S(1)} %copy-done.3, bf16[4,128,128]{2,1,0:T(8,128)(2,1)S(1)} %copy-done.4, f32[2]{0:T(128)S(1)} %copy-done.5), custom_call_target="tpu_custom_call" | custom-call | flops 67108864 | bytes 1048576 | tf_op jit(solution)/shard_map/pallas_call | solution.py:326
  27.6 0.8 %copy.8 = f32[2,2,64,512]{3,2,1,0:T(8,128)} copy(f32[2,2,64,512]{3,2,1,0:T(8,128)S(1)} %shard_map.64) | data formatting | bytes 1048576
Async XLA Ops:
  0.0 0.9 %copy-start = (bf16[2,2,64,512]{3,2,1,0:T(8,128)(2,1)S(1)}, bf16[2,2,64,512]{3,2,1,0:T(8,128)(2,1)}, u32[]{:S(2)}) copy-start(bf16[2,2,64,512]{3,2,1,0:T(8,128)(2,1)} %vel_hbm.1) | copy-start | bytes 786436
  1.0 0.9 %copy-start.1 = (bf16[2,2,64,512]{3,2,1,0:T(8,128)(2,1)S(1)}, bf16[2,2,64,512]{3,2,1,0:T(8,128)(2,1)}, u32[]{:S(2)}) copy-start(bf16[2,2,64,512]{3,2,1,0:T(8,128)(2,1)} %seed_hbm.1) | copy-start | bytes 786436
  1.9 0.9 %copy-start.2 = (s32[64,512]{1,0:T(8,128)S(1)}, s32[64,512]{1,0:T(8,128)}, u32[]{:S(2)}) copy-start(s32[64,512]{1,0:T(8,128)} %land_hbm.1) | copy-start | bytes 393220
  2.8 0.9 %copy-start.3 = (bf16[4,128,128]{2,1,0:T(8,128)(2,1)S(1)}, bf16[4,128,128]{2,1,0:T(8,128)(2,1)}, u32[]{:S(2)}) copy-start(bf16[4,128,128]{2,1,0:T(8,128)(2,1)} %ix_hbm.1) | copy-start | bytes 393220
  3.7 0.9 %copy-start.4 = (bf16[4,128,128]{2,1,0:T(8,128)(2,1)S(1)}, bf16[4,128,128]{2,1,0:T(8,128)(2,1)}, u32[]{:S(2)}) copy-start(bf16[4,128,128]{2,1,0:T(8,128)(2,1)} %iy_hbm.1) | copy-start | bytes 393220
  4.6 0.7 %copy-start.5 = (f32[2]{0:T(128)S(1)}, f32[2]{0:T(128)}, u32[]{:S(2)}) copy-start(f32[2]{0:T(128)} %w_hbm.1) | copy-start | bytes 28

commit v3 on v2

--- a/solution.py
+++ b/solution.py
@@ -325,14 +325,14 @@
     flops = 2 * 2 * n_cp * rows * side * BLK
     return pl.pallas_call(
         functools.partial(kernel, dims),
-        out_shape=jax.ShapeDtypeStruct(velocity.shape, F32),
+        out_shape=pltpu.VMEM(velocity.shape, F32),
         in_specs=[anywhere] * 6,
         out_specs=pl.BlockSpec(memory_space=pltpu.VMEM),
         scratch_shapes=scratch,
         cost_estimate=pl.CostEstimate(flops=flops, bytes_accessed=4 * velocity.size * 2, transcendentals=rows * side),
         compiler_params=pltpu.CompilerParams(
             collective_id=0, has_side_effects=True, vmem_limit_bytes=limit),
-    )(velocity, seed_adjoint, land_mask, inv_x, inv_y, weights)
+    )(*(pltpu.with_memory_space_constraint(a, pltpu.HBM) for a in (velocity, seed_adjoint, land_mask, inv_x, inv_y, weights)))
 
 
 def solution(mesh):

time: 28.6 us -> 23.2 us (0.81)
  local copies, waits for them, and re-layouts: 6.06 us -> 0.8 us
    unnamed x13 -> x1, local copies, waits for them, and re-layouts: 6.06 us -> 0.8 us
where the time goes in v3:
time: 23.2 us; the launch traced here: 23.1 us
  Pallas kernels  22.3 us (96%)
  local copies, waits for them, and re-layouts  0.8 us (3%)
    pallas_call x1, Pallas kernels, local(): pl.pallas_call(functools.partial(kernel, dims), out_shape=pltpu.VMEM(velo...  22.3 us
    unnamed x1, local copies, waits for them, and re-layouts  0.8 us

profile of v3, /device:TPU:0, one launch (start us, length us, event | category | flops | bytes accessed | tf_op | source)
XLA Modules:
  0.0 23.1 jit_solution(16283375558232179422)
XLA Ops:
  0.0 22.3 %shard_map.64 = f32[2,2,64,512]{3,2,1,0:T(8,128)S(1)} custom-call(bf16[2,2,64,512]{3,2,1,0:T(8,128)(2,1)} %vel_hbm.1, bf16[2,2,64,512]{3,2,1,0:T(8,128)(2,1)} %seed_hbm.1, s32[64,512]{1,0:T(8,128)} %land_hbm.1, bf16[4,128,128]{2,1,0:T(8,128)(2,1)} %ix_hbm.1, bf16[4,128,128]{2,1,0:T(8,128)(2,1)} %iy_hbm.1, f32[2]{0:T(128)} %w_hbm.1), custom_call_target="tpu_custom_call" | custom-call | flops 67108864 | bytes 1048576 | tf_op jit(solution)/shard_map/pallas_call | solution.py:326
  22.3 0.8 %copy.8 = f32[2,2,64,512]{3,2,1,0:T(8,128)} copy(f32[2,2,64,512]{3,2,1,0:T(8,128)S(1)} %shard_map.64) | data formatting | bytes 1048576

commit v4 on v3

--- a/solution.py
+++ b/solution.py
@@ -46,7 +46,7 @@
     vel, seed, land, ix, iy, w_ref,
     send, recv, wide, mask,
     sq_part, sq_send, sq_rs, sq_ag,
-    rhs, in_part, in_send, in_rs, in_ag, ca, cb,
+    rhs, in_part, in_send, in_rs, in_ag, in_all, ca, cb,
     load_sem, a2a_send, a2a_recv, sq_send_sem, sq_recv_sem, in_send_sem, in_recv_sem,
 ):
     n_con, n_grid, n_blk, con_local, rows, side = dims
@@ -74,14 +74,13 @@
     def a2a_copy(peer):
         return pltpu.make_async_remote_copy(
             src_ref=send.at[peer], dst_ref=recv.at[me],
-            send_sem=a2a_send.at[peer], recv_sem=a2a_recv.at[me],
+            send_sem=a2a_send.at[0], recv_sem=a2a_recv.at[own],
             device_id={"grid": peer}, device_id_type=MESH)
 
-    def a2a_arrival(peer):
-        return pltpu.make_async_remote_copy(
-            src_ref=send.at[peer], dst_ref=recv.at[peer],
-            send_sem=a2a_send.at[peer], recv_sem=a2a_recv.at[peer],
-            device_id={"grid": peer}, device_id_type=MESH)
+    def group(ref, send_sem, recv_sem):
+        return pltpu.make_async_remote_copy(
+            src_ref=ref, dst_ref=ref, send_sem=send_sem, recv_sem=recv_sem,
+            device_id={"con": lax.rem(zc + 1, n_con)}, device_id_type=MESH)
 
     def peer_in(step, slot):
         block = partner(own, step, n_blk)
@@ -132,22 +131,15 @@
         peer = lax.rem(zc + d, n_con)
         return pltpu.make_async_remote_copy(
             src_ref=sq_send.at[share_of(peer)], dst_ref=sq_rs.at[d - 1],
-            send_sem=sq_send_sem.at[0, d - 1], recv_sem=sq_recv_sem.at[0, d - 1],
+            send_sem=sq_send_sem.at[0], recv_sem=sq_recv_sem.at[0],
             device_id={"con": peer}, device_id_type=MESH)
 
     def sq_gather(d):
         peer = lax.rem(zc + d, n_con)
         return pltpu.make_async_remote_copy(
             src_ref=sq_ag.at[share_of(zc)], dst_ref=sq_ag.at[share_of(zc)],
-            send_sem=sq_send_sem.at[1, d - 1], recv_sem=sq_recv_sem.at[1, d - 1],
-            device_id={"con": peer}, device_id_type=MESH)
-
-    def sq_gathered(d):
-        source = lax.rem(zc + n_con - d, n_con)
-        return pltpu.make_async_remote_copy(
-            src_ref=sq_ag.at[share_of(zc)], dst_ref=sq_ag.at[share_of(source)],
-            send_sem=sq_send_sem.at[1, d - 1], recv_sem=sq_recv_sem.at[1, d - 1],
-            device_id={"con": source}, device_id_type=MESH)
+            send_sem=sq_send_sem.at[1], recv_sem=sq_recv_sem.at[1],
+            device_id={"con": peer}, device_id_type=MESH)
 
     for d in range(1, n_con):
         sq_scatter(d).start()
@@ -179,8 +171,7 @@
 
     steps(0, n_blk, prepare)
 
-    for d in range(1, n_con):
-        sq_scatter(d).wait_recv()
+    group(sq_rs, sq_send_sem.at[0], sq_recv_sem.at[0]).wait_recv()
     total = sq_part[share_of(zc)]
     for d in range(1, n_con):
         total = total + sq_rs[d - 1].astype(F32)
@@ -188,31 +179,34 @@
     for d in range(1, n_con):
         sq_gather(d).start()
 
-    def in_scatter(step, d):
-        peer = lax.rem(zc + d, n_con)
-        return pltpu.make_async_remote_copy(
-            src_ref=in_send.at[step, share_of(peer)], dst_ref=in_rs.at[step, d - 1],
-            send_sem=in_send_sem.at[0, step, d - 1], recv_sem=in_recv_sem.at[0, step, d - 1],
-            device_id={"con": peer}, device_id_type=MESH)
-
-    def in_gather(step, d):
-        peer = lax.rem(zc + d, n_con)
-        return pltpu.make_async_remote_copy(
-            src_ref=in_ag.at[step, share_of(zc)], dst_ref=in_ag.at[step, share_of(zc)],
-            send_sem=in_send_sem.at[1, step, d - 1], recv_sem=in_recv_sem.at[1, step, d - 1],
-            device_id={"con": peer}, device_id_type=MESH)
-
-    def in_gathered(step, d):
-        source = lax.rem(zc + n_con - d, n_con)
-        return pltpu.make_async_remote_copy(
-            src_ref=in_ag.at[step, share_of(zc)], dst_ref=in_ag.at[step, share_of(source)],
-            send_sem=in_send_sem.at[1, step, d - 1], recv_sem=in_recv_sem.at[1, step, d - 1],
-            device_id={"con": source}, device_id_type=MESH)
-
-    def solve_y(step, waits):
-        for peer in waits:
-            a2a_arrival(peer).wait_recv()
+    middle, last = n_blk // 2, n_blk - 1
+    shared = [(j, a, b) for j, (a, b) in enumerate(((0, middle), (middle, last))) if b > a]
+
+    def in_scatter(j, a, b, d):
+        peer = lax.rem(zc + d, n_con)
+        return pltpu.make_async_remote_copy(
+            src_ref=in_send.at[a:b, share_of(peer)], dst_ref=in_rs.at[d - 1, a:b],
+            send_sem=in_send_sem.at[0], recv_sem=in_recv_sem.at[0, j],
+            device_id={"con": peer}, device_id_type=MESH)
+
+    def in_gather(j, a, b, d):
+        peer = lax.rem(zc + d, n_con)
+        return pltpu.make_async_remote_copy(
+            src_ref=in_ag.at[a:b, share_of(zc)], dst_ref=in_ag.at[a:b, share_of(zc)],
+            send_sem=in_send_sem.at[1], recv_sem=in_recv_sem.at[1, j],
+            device_id={"con": peer}, device_id_type=MESH)
+
+    def in_straight(d):
+        peer = lax.rem(zc + d, n_con)
+        return pltpu.make_async_remote_copy(
+            src_ref=in_send.at[last], dst_ref=in_all.at[d - 1],
+            send_sem=in_send_sem.at[2], recv_sem=in_recv_sem.at[0, 2],
+            device_id={"con": peer}, device_id_type=MESH)
+
+    def solve_y(step, arriving=pack):
         block = partner(own, step, n_blk)
+        if arriving:
+            group(recv.at[pl.ds(block * pack, arriving)], a2a_send.at[0], a2a_recv.at[block]).wait_recv()
         cols = lanes(block)
         weight = wide[block]
         keep = mask[block]
@@ -229,30 +223,34 @@
             total = total + value * vel[cp // 2, cp % 2, :, cols].astype(F32)
         in_part[step] = total
         in_send[step] = total.astype(BF16)
+
+    def scatter_inner(j, a, b):
         for d in range(1, n_con):
-            in_scatter(step, d).start()
-
-    def reduce_inner(step):
+            in_scatter(j, a, b, d).start()
+
+    def reduce_inner(j, a, b):
+        group(in_rs.at[:, a:b], in_send_sem.at[0], in_recv_sem.at[0, j]).wait_recv()
+        mine = in_part[a:b, share_of(zc)]
         for d in range(1, n_con):
-            in_scatter(step, d).wait_recv()
-        mine = in_part[step, share_of(zc)]
+            mine = mine + in_rs[d - 1, a:b].astype(F32)
+        in_ag[a:b, share_of(zc)] = mine.astype(BF16)
         for d in range(1, n_con):
-            mine = mine + in_rs[step, d - 1].astype(F32)
-        in_ag[step, share_of(zc)] = mine.astype(BF16)
-        for d in range(1, n_con):
-            in_gather(step, d).start()
-
-    solve_y(0, [own * pack + lax.rem(core + slot, pack) for slot in range(1, pack)])
-
-    def step_y(step):
-        solve_y(step, [peer_in(step, slot) for slot in range(pack)])
-        reduce_inner(step - 1)
-
-    steps(1, n_blk, step_y)
-    reduce_inner(n_blk - 1)
-
-    for d in range(1, n_con):
-        sq_gathered(d).wait_recv()
+            in_gather(j, a, b, d).start()
+
+    solve_y(0, pack - 1)
+    for place, (j, a, b) in enumerate(shared):
+        steps(max(a, 1), b, solve_y)
+        scatter_inner(j, a, b)
+        if place:
+            reduce_inner(*shared[place - 1])
+    if last > 0:
+        solve_y(last)
+    for d in range(1, n_con):
+        in_straight(d).start()
+    if shared:
+        reduce_inner(*shared[-1])
+
+    group(sq_rs, sq_send_sem.at[1], sq_recv_sem.at[1]).wait_recv()
 
     def factors(block):
         cols = lanes(block)
@@ -264,37 +262,37 @@
 
     steps(0, n_blk, factors)
 
-    def finish(step):
-        for d in range(1, n_con):
-            in_gathered(step, d).wait_recv()
+    group(send.at[0:n_grid - 1], a2a_send.at[0], a2a_recv.at[0]).wait_send()
+    group(sq_rs, sq_send_sem.at[0], sq_recv_sem.at[0]).wait_send()
+    group(sq_rs, sq_send_sem.at[1], sq_recv_sem.at[1]).wait_send()
+    if shared:
+        group(in_rs, in_send_sem.at[0], in_recv_sem.at[0, 0]).wait_send()
+
+    def finish(step, inner):
         cols = lanes(partner(own, step, n_blk))
         first = ca[:, cols]
-        second = cb[:, cols] * in_ag[step].astype(F32)
+        second = cb[:, cols] * inner
         for c in range(con_local):
             scaled = w_ref[c] * second
             for p in range(2):
                 out_ref[c, p, :, cols] = first * rhs[2 * c + p, :, cols] + scaled * vel[c, p, :, cols].astype(F32)
 
-    steps(0, n_blk, finish)
-
-    for slot in range(1, pack):
-        a2a_copy(own * pack + lax.rem(core + slot, pack)).wait_send()
-
-    def left(step):
-        for slot in range(pack):
-            a2a_copy(peer_in(step, slot)).wait_send()
-
-    steps(1, n_blk, left)
-    for d in range(1, n_con):
-        sq_scatter(d).wait_send()
-        sq_gather(d).wait_send()
-
-    def in_left(step):
-        for d in range(1, n_con):
-            in_scatter(step, d).wait_send()
-            in_gather(step, d).wait_send()
-
-    steps(0, n_blk, in_left)
+    def finish_shared(j, a, b):
+        group(in_rs.at[:, a:b], in_send_sem.at[1], in_recv_sem.at[1, j]).wait_recv()
+        steps(a, b, lambda step: finish(step, in_ag[step].astype(F32)))
+
+    for part in shared[:-1]:
+        finish_shared(*part)
+    group(in_all, in_send_sem.at[2], in_recv_sem.at[0, 2]).wait_recv()
+    total = in_part[last]
+    for d in range(1, n_con):
+        total = total + in_all[d - 1].astype(F32)
+    finish(last, total)
+    for part in shared[-1:]:
+        finish_shared(*part)
+    if shared:
+        group(in_rs, in_send_sem.at[1], in_recv_sem.at[0, 0]).wait_send()
+    group(in_all, in_send_sem.at[2], in_recv_sem.at[0, 2]).wait_send()
 
 
 def local(n_con, n_grid, velocity, seed_adjoint, land_mask, inv_x, inv_y, weights):
@@ -314,12 +312,12 @@
         vm((n_blk, pack * BLK, pack * BLK), BF16), vm((n_blk, rows, pack * BLK), BF16),
         vm((rows, side), F32), vm((rows, side), BF16), vm((peers, share, side), BF16), vm((rows, side), BF16),
         vm((n_cp, rows, side), F32), vm((n_blk, rows, BLK), F32), vm((n_blk, rows, BLK), BF16),
-        vm((n_blk, peers, share, BLK), BF16), vm((n_blk, rows, BLK), BF16),
+        vm((peers, max(n_blk - 1, 1), share, BLK), BF16), vm((n_blk, rows, BLK), BF16),
+        vm((peers, rows, BLK), BF16),
         vm((rows, side), F32), vm((rows, side), F32),
-        sem((6,)), sem((n_grid,)), sem((n_grid,)),
-        sem((2, peers)), sem((2, peers)), sem((2, n_blk, peers)), sem((2, n_blk, peers)),
+        sem((6,)), sem((1,)), sem((n_blk,)), sem((2,)), sem((2,)), sem((3,)), sem((2, 3)),
     ]
-    held = sum(math.prod(spec.shape) * jnp.dtype(spec.dtype).itemsize for spec in scratch[:21])
+    held = sum(math.prod(spec.shape) * jnp.dtype(spec.dtype).itemsize for spec in scratch[:22])
     limit = held + velocity.size * 4 + max(4 << 20, velocity.size * 4)
     anywhere = pl.BlockSpec(memory_space=pltpu.HBM)
     flops = 2 * 2 * n_cp * rows * side * BLK

time: 23.2 us -> 19.8 us (0.85)
  Pallas kernels: 22.3 us -> 18.8 us
    pallas_call x1, Pallas kernels: 22.3 us -> 18.8 us  [local(): pl.pallas_call(functools.partial(kernel, dims), out_shape=pltpu.VMEM(velo...]
where the time goes in v4:
time: 19.8 us; the launch traced here: 19.6 us
  Pallas kernels  18.8 us (95%)
  local copies, waits for them, and re-layouts  0.8 us (4%)
    pallas_call x1, Pallas kernels, local(): pl.pallas_call(functools.partial(kernel, dims), out_shape=pltpu.VMEM(velo...  18.8 us
    unnamed x1, local copies, waits for them, and re-layouts  0.8 us

profile of v4, /device:TPU:0, one launch (start us, length us, event | category | flops | bytes accessed | tf_op | source)
XLA Modules:
  0.0 19.6 jit_solution(2536872016175429746)
XLA Ops:
  0.0 18.8 %shard_map.64 = f32[2,2,64,512]{3,2,1,0:T(8,128)S(1)} custom-call(bf16[2,2,64,512]{3,2,1,0:T(8,128)(2,1)} %vel_hbm.1, bf16[2,2,64,512]{3,2,1,0:T(8,128)(2,1)} %seed_hbm.1, s32[64,512]{1,0:T(8,128)} %land_hbm.1, bf16[4,128,128]{2,1,0:T(8,128)(2,1)} %ix_hbm.1, bf16[4,128,128]{2,1,0:T(8,128)(2,1)} %iy_hbm.1, f32[2]{0:T(128)} %w_hbm.1), custom_call_target="tpu_custom_call" | custom-call | flops 67108864 | bytes 1048576 | tf_op jit(solution)/shard_map/pallas_call | solution.py:324
  18.8 0.8 %copy.8 = f32[2,2,64,512]{3,2,1,0:T(8,128)} copy(f32[2,2,64,512]{3,2,1,0:T(8,128)S(1)} %shard_map.64) | data formatting | bytes 1048576

commit v5 on v4

--- a/solution.py
+++ b/solution.py
@@ -59,17 +59,25 @@
     own = lax.div(me, pack)
     core = lax.rem(me, pack)
 
+    loads = []
+
+    def load(src, dst):
+        copy = pltpu.make_async_copy(src, dst, load_sem.at[len(loads)])
+        copy.start()
+        loads.append(copy)
+
+    load(seed_hbm, seed)
+    load(ix_hbm, ix)
     barrier = pltpu.get_barrier_semaphore()
     for d in range(1, n_grid):
         pl.semaphore_signal(barrier, inc=1, device_id={"grid": lax.rem(me + d, n_grid)}, device_id_type=MESH)
     for d in range(1, n_con):
         pl.semaphore_signal(barrier, inc=1, device_id={"con": lax.rem(zc + d, n_con)}, device_id_type=MESH)
 
-    loads = []
-    for i, (src, dst) in enumerate(((seed_hbm, seed), (ix_hbm, ix), (vel_hbm, vel), (w_hbm, w_ref), (iy_hbm, iy), (land_hbm, land))):
-        copy = pltpu.make_async_copy(src, dst, load_sem.at[i])
-        copy.start()
-        loads.append(copy)
+    load(vel_hbm, vel)
+    load(w_hbm, w_ref)
+    load(iy_hbm, iy)
+    load(land_hbm, land)
 
     def a2a_copy(peer):
         return pltpu.make_async_remote_copy(
@@ -179,8 +187,8 @@
     for d in range(1, n_con):
         sq_gather(d).start()
 
-    middle, last = n_blk // 2, n_blk - 1
-    shared = [(j, a, b) for j, (a, b) in enumerate(((0, middle), (middle, last))) if b > a]
+    last = n_blk - 1
+    shared = [(0, 0, last)] if last else []
 
     def in_scatter(j, a, b, d):
         peer = lax.rem(zc + d, n_con)
@@ -281,14 +289,12 @@
         group(in_rs.at[:, a:b], in_send_sem.at[1], in_recv_sem.at[1, j]).wait_recv()
         steps(a, b, lambda step: finish(step, in_ag[step].astype(F32)))
 
-    for part in shared[:-1]:
-        finish_shared(*part)
     group(in_all, in_send_sem.at[2], in_recv_sem.at[0, 2]).wait_recv()
     total = in_part[last]
     for d in range(1, n_con):
         total = total + in_all[d - 1].astype(F32)
     finish(last, total)
-    for part in shared[-1:]:
+    for part in shared:
         finish_shared(*part)
     if shared:
         group(in_rs, in_send_sem.at[1], in_recv_sem.at[0, 0]).wait_send()

time: 19.8 us -> 19.8 us (level)
  no operation moved by 1% of the time
where the time goes in v5:
time: 19.8 us; the launch traced here: 19.7 us
  Pallas kernels  18.9 us (95%)
  local copies, waits for them, and re-layouts  0.8 us (4%)
    pallas_call x1, Pallas kernels, local(): pl.pallas_call(functools.partial(kernel, dims), out_shape=pltpu.VMEM(velo...  18.9 us
    unnamed x1, local copies, waits for them, and re-layouts  0.8 us

profile of v5, /device:TPU:0, one launch (start us, length us, event | category | flops | bytes accessed | tf_op | source)
XLA Modules:
  0.0 19.7 jit_solution(2621881849024423704)
XLA Ops:
  0.0 18.9 %shard_map.64 = f32[2,2,64,512]{3,2,1,0:T(8,128)S(1)} custom-call(bf16[2,2,64,512]{3,2,1,0:T(8,128)(2,1)} %vel_hbm.1, bf16[2,2,64,512]{3,2,1,0:T(8,128)(2,1)} %seed_hbm.1, s32[64,512]{1,0:T(8,128)} %land_hbm.1, bf16[4,128,128]{2,1,0:T(8,128)(2,1)} %ix_hbm.1, bf16[4,128,128]{2,1,0:T(8,128)(2,1)} %iy_hbm.1, f32[2]{0:T(128)} %w_hbm.1), custom_call_target="tpu_custom_call" | custom-call | flops 67108864 | bytes 1048576 | tf_op jit(solution)/shard_map/pallas_call | solution.py:330
  18.9 0.8 %copy.8 = f32[2,2,64,512]{3,2,1,0:T(8,128)} copy(f32[2,2,64,512]{3,2,1,0:T(8,128)S(1)} %shard_map.64) | data formatting | bytes 1048576

commit v6 on v5

--- a/solution.py
+++ b/solution.py
@@ -46,7 +46,7 @@
     vel, seed, land, ix, iy, w_ref,
     send, recv, wide, mask,
     sq_part, sq_send, sq_rs, sq_ag,
-    rhs, in_part, in_send, in_rs, in_ag, in_all, ca, cb,
+    rhs, in_part, in_send, in_rs, in_ag, ca, cb,
     load_sem, a2a_send, a2a_recv, sq_send_sem, sq_recv_sem, in_send_sem, in_recv_sem,
 ):
     n_con, n_grid, n_blk, con_local, rows, side = dims
@@ -179,42 +179,26 @@
 
     steps(0, n_blk, prepare)
 
-    group(sq_rs, sq_send_sem.at[0], sq_recv_sem.at[0]).wait_recv()
-    total = sq_part[share_of(zc)]
-    for d in range(1, n_con):
-        total = total + sq_rs[d - 1].astype(F32)
-    sq_ag[share_of(zc)] = total.astype(BF16)
-    for d in range(1, n_con):
-        sq_gather(d).start()
-
-    last = n_blk - 1
-    shared = [(0, 0, last)] if last else []
-
-    def in_scatter(j, a, b, d):
+    def in_scatter(d):
         peer = lax.rem(zc + d, n_con)
         return pltpu.make_async_remote_copy(
-            src_ref=in_send.at[a:b, share_of(peer)], dst_ref=in_rs.at[d - 1, a:b],
-            send_sem=in_send_sem.at[0], recv_sem=in_recv_sem.at[0, j],
+            src_ref=in_send.at[:, share_of(peer)], dst_ref=in_rs.at[d - 1],
+            send_sem=in_send_sem.at[0], recv_sem=in_recv_sem.at[0],
             device_id={"con": peer}, device_id_type=MESH)
 
-    def in_gather(j, a, b, d):
+    def in_gather(d):
         peer = lax.rem(zc + d, n_con)
         return pltpu.make_async_remote_copy(
-            src_ref=in_ag.at[a:b, share_of(zc)], dst_ref=in_ag.at[a:b, share_of(zc)],
-            send_sem=in_send_sem.at[1], recv_sem=in_recv_sem.at[1, j],
+            src_ref=in_ag.at[:, share_of(zc)], dst_ref=in_ag.at[:, share_of(zc)],
+            send_sem=in_send_sem.at[1], recv_sem=in_recv_sem.at[1],
             device_id={"con": peer}, device_id_type=MESH)
 
-    def in_straight(d):
-        peer = lax.rem(zc + d, n_con)
-        return pltpu.make_async_remote_copy(
-            src_ref=in_send.at[last], dst_ref=in_all.at[d - 1],
-            send_sem=in_send_sem.at[2], recv_sem=in_recv_sem.at[0, 2],
-            device_id={"con": peer}, device_id_type=MESH)
-
-    def solve_y(step, arriving=pack):
+    def arrive(step, count=pack):
         block = partner(own, step, n_blk)
-        if arriving:
-            group(recv.at[pl.ds(block * pack, arriving)], a2a_send.at[0], a2a_recv.at[block]).wait_recv()
+        group(recv.at[pl.ds(block * pack, count)], a2a_send.at[0], a2a_recv.at[block]).wait_recv()
+
+    def solve_y(step):
+        block = partner(own, step, n_blk)
         cols = lanes(block)
         weight = wide[block]
         keep = mask[block]
@@ -232,31 +216,29 @@
         in_part[step] = total
         in_send[step] = total.astype(BF16)
 
-    def scatter_inner(j, a, b):
-        for d in range(1, n_con):
-            in_scatter(j, a, b, d).start()
-
-    def reduce_inner(j, a, b):
-        group(in_rs.at[:, a:b], in_send_sem.at[0], in_recv_sem.at[0, j]).wait_recv()
-        mine = in_part[a:b, share_of(zc)]
-        for d in range(1, n_con):
-            mine = mine + in_rs[d - 1, a:b].astype(F32)
-        in_ag[a:b, share_of(zc)] = mine.astype(BF16)
-        for d in range(1, n_con):
-            in_gather(j, a, b, d).start()
-
-    solve_y(0, pack - 1)
-    for place, (j, a, b) in enumerate(shared):
-        steps(max(a, 1), b, solve_y)
-        scatter_inner(j, a, b)
-        if place:
-            reduce_inner(*shared[place - 1])
-    if last > 0:
-        solve_y(last)
-    for d in range(1, n_con):
-        in_straight(d).start()
-    if shared:
-        reduce_inner(*shared[-1])
+    if pack > 1:
+        arrive(0, pack - 1)
+    solve_y(0)
+
+    group(sq_rs, sq_send_sem.at[0], sq_recv_sem.at[0]).wait_recv()
+    total = sq_part[share_of(zc)]
+    for d in range(1, n_con):
+        total = total + sq_rs[d - 1].astype(F32)
+    sq_ag[share_of(zc)] = total.astype(BF16)
+    for d in range(1, n_con):
+        sq_gather(d).start()
+
+    steps(1, n_blk, arrive)
+    steps(1, n_blk, solve_y)
+    for d in range(1, n_con):
+        in_scatter(d).start()
+    group(in_rs, in_send_sem.at[0], in_recv_sem.at[0]).wait_recv()
+    mine = in_part[:, share_of(zc)]
+    for d in range(1, n_con):
+        mine = mine + in_rs[d - 1].astype(F32)
+    in_ag[:, share_of(zc)] = mine.astype(BF16)
+    for d in range(1, n_con):
+        in_gather(d).start()
 
     group(sq_rs, sq_send_sem.at[1], sq_recv_sem.at[1]).wait_recv()
 
@@ -273,32 +255,20 @@
     group(send.at[0:n_grid - 1], a2a_send.at[0], a2a_recv.at[0]).wait_send()
     group(sq_rs, sq_send_sem.at[0], sq_recv_sem.at[0]).wait_send()
     group(sq_rs, sq_send_sem.at[1], sq_recv_sem.at[1]).wait_send()
-    if shared:
-        group(in_rs, in_send_sem.at[0], in_recv_sem.at[0, 0]).wait_send()
-
-    def finish(step, inner):
+    group(in_rs, in_send_sem.at[0], in_recv_sem.at[0]).wait_send()
+
+    def finish(step):
         cols = lanes(partner(own, step, n_blk))
         first = ca[:, cols]
-        second = cb[:, cols] * inner
+        second = cb[:, cols] * in_ag[step].astype(F32)
         for c in range(con_local):
             scaled = w_ref[c] * second
             for p in range(2):
                 out_ref[c, p, :, cols] = first * rhs[2 * c + p, :, cols] + scaled * vel[c, p, :, cols].astype(F32)
 
-    def finish_shared(j, a, b):
-        group(in_rs.at[:, a:b], in_send_sem.at[1], in_recv_sem.at[1, j]).wait_recv()
-        steps(a, b, lambda step: finish(step, in_ag[step].astype(F32)))
-
-    group(in_all, in_send_sem.at[2], in_recv_sem.at[0, 2]).wait_recv()
-    total = in_part[last]
-    for d in range(1, n_con):
-        total = total + in_all[d - 1].astype(F32)
-    finish(last, total)
-    for part in shared:
-        finish_shared(*part)
-    if shared:
-        group(in_rs, in_send_sem.at[1], in_recv_sem.at[0, 0]).wait_send()
-    group(in_all, in_send_sem.at[2], in_recv_sem.at[0, 2]).wait_send()
+    group(in_rs, in_send_sem.at[1], in_recv_sem.at[1]).wait_recv()
+    steps(0, n_blk, finish)
+    group(in_rs, in_send_sem.at[1], in_recv_sem.at[1]).wait_send()
 
 
 def local(n_con, n_grid, velocity, seed_adjoint, land_mask, inv_x, inv_y, weights):
@@ -318,12 +288,11 @@
         vm((n_blk, pack * BLK, pack * BLK), BF16), vm((n_blk, rows, pack * BLK), BF16),
         vm((rows, side), F32), vm((rows, side), BF16), vm((peers, share, side), BF16), vm((rows, side), BF16),
         vm((n_cp, rows, side), F32), vm((n_blk, rows, BLK), F32), vm((n_blk, rows, BLK), BF16),
-        vm((peers, max(n_blk - 1, 1), share, BLK), BF16), vm((n_blk, rows, BLK), BF16),
-        vm((peers, rows, BLK), BF16),
+        vm((peers, n_blk, share, BLK), BF16), vm((n_blk, rows, BLK), BF16),
         vm((rows, side), F32), vm((rows, side), F32),
-        sem((6,)), sem((1,)), sem((n_blk,)), sem((2,)), sem((2,)), sem((3,)), sem((2, 3)),
+        sem((6,)), sem((1,)), sem((n_blk,)), sem((2,)), sem((2,)), sem((2,)), sem((2,)),
     ]
-    held = sum(math.prod(spec.shape) * jnp.dtype(spec.dtype).itemsize for spec in scratch[:22])
+    held = sum(math.prod(spec.shape) * jnp.dtype(spec.dtype).itemsize for spec in scratch[:21])
     limit = held + velocity.size * 4 + max(4 << 20, velocity.size * 4)
     anywhere = pl.BlockSpec(memory_space=pltpu.HBM)
     flops = 2 * 2 * n_cp * rows * side * BLK

time: 19.8 us -> 20 us (1.010)
  no operation moved by 1% of the time
where the time goes in v6:
time: 20 us; the launch traced here: 19.8 us
  Pallas kernels  19 us (95%)
  local copies, waits for them, and re-layouts  0.8 us (4%)
    pallas_call x1, Pallas kernels, local(): pl.pallas_call(functools.partial(kernel, dims), out_shape=pltpu.VMEM(velo...  19 us
    unnamed x1, local copies, waits for them, and re-layouts  0.8 us

profile of v6, /device:TPU:0, one launch (start us, length us, event | category | flops | bytes accessed | tf_op | source)
XLA Modules:
  0.0 19.8 jit_solution(9234453660466050644)
XLA Ops:
  0.0 19.0 %shard_map.64 = f32[2,2,64,512]{3,2,1,0:T(8,128)S(1)} custom-call(bf16[2,2,64,512]{3,2,1,0:T(8,128)(2,1)} %vel_hbm.1, bf16[2,2,64,512]{3,2,1,0:T(8,128)(2,1)} %seed_hbm.1, s32[64,512]{1,0:T(8,128)} %land_hbm.1, bf16[4,128,128]{2,1,0:T(8,128)(2,1)} %ix_hbm.1, bf16[4,128,128]{2,1,0:T(8,128)(2,1)} %iy_hbm.1, f32[2]{0:T(128)} %w_hbm.1), custom_call_target="tpu_custom_call" | custom-call | flops 67108864 | bytes 1048576 | tf_op jit(solution)/shard_map/pallas_call | solution.py:299
  19.0 0.8 %copy.8 = f32[2,2,64,512]{3,2,1,0:T(8,128)} copy(f32[2,2,64,512]{3,2,1,0:T(8,128)S(1)} %shard_map.64) | data formatting | bytes 1048576

commit v7 on v5

--- a/solution.py
+++ b/solution.py
@@ -26,7 +26,7 @@
 
 
 def steps(first, stop, body):
-    if stop - first <= 8:
+    if stop - first <= 1:
         for step in range(first, stop):
             body(step)
     else:

time: 19.8 us -> 19.9 us (level)
  no operation moved by 1% of the time
where the time goes in v7:
time: 19.9 us; the launch traced here: 19.8 us
  Pallas kernels  18.9 us (95%)
  local copies, waits for them, and re-layouts  0.8 us (4%)
    pallas_call x1, Pallas kernels, local(): pl.pallas_call(functools.partial(kernel, dims), out_shape=pltpu.VMEM(velo...  18.9 us
    unnamed x1, local copies, waits for them, and re-layouts  0.8 us

profile of v7, /device:TPU:0, one launch (start us, length us, event | category | flops | bytes accessed | tf_op | source)
XLA Modules:
  0.0 19.8 jit_solution(7994269627403806827)
XLA Ops:
  0.0 18.9 %shard_map.64 = f32[2,2,64,512]{3,2,1,0:T(8,128)S(1)} custom-call(bf16[2,2,64,512]{3,2,1,0:T(8,128)(2,1)} %vel_hbm.1, bf16[2,2,64,512]{3,2,1,0:T(8,128)(2,1)} %seed_hbm.1, s32[64,512]{1,0:T(8,128)} %land_hbm.1, bf16[4,128,128]{2,1,0:T(8,128)(2,1)} %ix_hbm.1, bf16[4,128,128]{2,1,0:T(8,128)(2,1)} %iy_hbm.1, f32[2]{0:T(128)} %w_hbm.1), custom_call_target="tpu_custom_call" | custom-call | flops 67108864 | bytes 1048576 | tf_op jit(solution)/shard_map/pallas_call | solution.py:330
  19.0 0.8 %copy.8 = f32[2,2,64,512]{3,2,1,0:T(8,128)} copy(f32[2,2,64,512]{3,2,1,0:T(8,128)S(1)} %shard_map.64) | data formatting | bytes 1048576
